TPU v7x, 256 devices: a whole 4x4x8 slice. The times are simulated.
256 devices in a mesh: rows: 64 (over x, y_lo, z), cols: 4 (over y_hi, core).
Axes of the slice: x: 4, y: 4 (y_hi: 2, y_lo: 2; y = y_hi * 2 + y_lo), z: 8, core: 2. Of those that a mesh axis runs over, the one named last changes fastest.
Arguments:
- right_side: float32 [32, 131072], P(None, ('rows', 'cols')), may hold values from -6 to 6
- local_inverse: float32 [64, 4, 1024, 1024], P('rows', 'cols'), may hold values from -1 to 2.5, as said below
- modes: float32 [64, 4, 64, 1024], P('rows', 'cols'), may hold values from -0.1875 to 0.1875
- coarse_inverse: float32 [16384, 16384], P('rows', 'cols'), may hold values from -1 to 2.5, as said below
- stiff_diag: float32 [64, 4, 1024], P('rows', 'cols'), may hold values from 1 to 4
- nbr_index: int32 [64, 4, 80, 1024], P('rows', 'cols'), may hold values from 0 to 1023
- nbr_coef: float32 [64, 4, 80, 1024], P('rows', 'cols'), may hold values from -0.625 to 0.625
- send_rows: int32 [64, 4, 4, 128], P('rows', 'cols'), may hold values from 0 to 511
Outputs:
- solution: float32 [32, 131072], P(None, ('rows', 'cols'))
- residual: float32 [32, 131072], P(None, ('rows', 'cols'))
Inputs may be any that keep to these rules, and one draw needn't show every extreme that they name: `local_inverse`: each subdomain inverse has a diagonal between 0.25 and 2 and small off-diagonal entries. `coarse_inverse`: a diagonal between 0.25 and 2 at entries whose row and column name the same coarse unknown, small entries elsewhere.
All inputs are finite; a program needn't handle non-finite values.
Results may differ from a plain program's by a relative error of at most 0.00013.
Values sent between devices are 32-bit elements; how exact they have to be, the bound alone decides.
A program may use at most 128 MiB of HBM per device.

v0:
```python
import jax
import jax.numpy as jnp
from jax import lax
from jax.sharding import PartitionSpec as P


def from_behind(block, axis, distance):
    devices = range(lax.axis_size(axis))
    route = [(i - distance, i) for i in devices if i - distance in devices]
    return lax.ppermute(block, axis, route)


def along_rows(block, offset):
    return from_behind(block, "rows", offset)


def along_cols(block, offset):
    return from_behind(block, "cols", offset)


def extend(owned, sends):
    picked = [owned[:, sends[e]] for e in range(4)]
    first = along_rows(picked[0], 1)
    second = along_rows(picked[1], -1)
    third = along_cols(picked[2], 1)
    fourth = along_cols(picked[3], -1)
    return jnp.concatenate([owned, first, second, third, fourth], axis=1)


def fold(sub, sends, own_count, block_rows):
    owned = sub[:, :own_count]
    bands = [
        sub[:, own_count + e * block_rows : own_count + (e + 1) * block_rows] for e in range(4)
    ]
    backs = [
        along_rows(bands[0], -1),
        along_rows(bands[1], 1),
        along_cols(bands[2], -1),
        along_cols(bands[3], 1),
    ]
    for e in range(4):
        owned = owned.at[:, sends[e]].add(backs[e])
    return owned


def coarse_apply(restricted, coarse_block):
    highest = lax.Precision.HIGHEST
    partial_sum = lax.dot_general(
        lax.all_gather(restricted, "rows", axis=1, tiled=True),
        coarse_block,
        (((1,), (1,)), ((), ())),
        precision=highest,
        preferred_element_type=jnp.float32,
    )
    return lax.psum_scatter(partial_sum, "cols", scatter_dimension=1, tiled=True)


def couple(sub, diag, index, coef):
    coupled = diag[None, :] * sub
    count = index.shape[0]
    group = min(16, count)
    for begin in range(0, count, group):
        finish = min(begin + group, count)
        nearby = sub[:, index[begin:finish]]
        coupled = coupled + jnp.sum(nearby * coef[None, begin:finish, :], axis=1)
    return coupled


def body(
    right_side, local_inverse, modes, coarse_inverse, stiff_diag, nbr_index, nbr_coef, send_rows
):
    highest = lax.Precision.HIGHEST
    inverse = local_inverse[0, 0]
    basis = modes[0, 0]
    diag = stiff_diag[0, 0]
    index = nbr_index[0, 0]
    coef = nbr_coef[0, 0]
    sends = send_rows[0, 0]
    own_count = right_side.shape[1]
    block_rows = sends.shape[1]

    def precondition(resid):
        sub = extend(resid, sends)
        local = lax.dot_general(
            sub,
            inverse,
            (((1,), (1,)), ((), ())),
            precision=highest,
            preferred_element_type=jnp.float32,
        )
        restricted = lax.dot_general(
            sub,
            basis,
            (((1,), (1,)), ((), ())),
            precision=highest,
            preferred_element_type=jnp.float32,
        )
        coarse = coarse_apply(restricted, coarse_inverse)
        local = local + jnp.dot(
            coarse, basis, precision=highest, preferred_element_type=jnp.float32
        )
        return fold(local, sends, own_count, block_rows)

    first = precondition(right_side)
    sub = extend(first, sends)
    coupled = couple(sub, diag, index, coef)
    image = fold(coupled, sends, own_count, block_rows)
    residual = right_side - image
    solution = first + precondition(residual)
    return (solution, residual)


def solution(mesh):
    in_specs = (
        P(None, ("rows", "cols")),
        P("rows", "cols", None, None),
        P("rows", "cols", None, None),
        P("rows", "cols"),
        P("rows", "cols", None),
        P("rows", "cols", None, None),
        P("rows", "cols", None, None),
        P("rows", "cols", None, None),
    )
    out_specs = (P(None, ("rows", "cols")), P(None, ("rows", "cols")))
    return jax.shard_map(body, mesh=mesh, in_specs=in_specs, out_specs=out_specs, check_vma=False)
```

profile of v0, /device:TPU:120, one launch (start us, length us, event | category | flops | bytes accessed | tf_op | source)
XLA Modules:
  0.0 825.7 jit_solution(2240018692300086383)
XLA Ops:
  9.7 5.0 collective-permute-start
  20.5 5.1 collective-permute-start.3
  28.4 136.5 %all-gather = f32[64,64,32]{1,2,0:T(8,128)S(1)} all-gather(f32[1,64,32]{1,2,0:T(8,128)S(1)} %convolution_bitcast_fusion.3), channel_id=1, replica_groups=mesh['rows'=64,'cols'=4] {'rows'}, dimensions={0}, use_global_device_ids=true | all-gather | bytes 532480 | tf_op jit(solution)/shard_map/all_gather | solution.py:49
  165.9 5.8 convolution_bitcast_fusion.1
  171.7 49.3 %reduce-scatter.7.cloned.1.call-done = f32[64,32]{1,0:T(8,128)} async-done(((f32[256,32]{1,0:T(8,128)}), f32[64,32]{1,0:T(8,128)}) %reduce-scatter.7.cloned.1.call-update) | async-done | bytes 8208
  222.1 6.0 fusion.4
  230.1 5.1 collective-permute-start.6
  242.0 4.7 collective-permute-done.4
  263.1 5.3 collective-permute-start.11
  270.1 54.4 %gather_fusion.12 = f32[16384,32]{1,0:T(8,128)} fusion(f32[32,1024]{0,1:T(8,128)S(1)} %constant_dynamic-update-slice_fusion.5, s32[16384]{0:T(1024)S(1)} %broadcast_clamp_fusion), kind=kCustom, calls=%fused_computation.12 | custom fusion | bytes 4259840 | tf_op jit(solution)/shard_map/gather | solution.py:64
  324.5 54.4 %gather_fusion.11 = f32[16384,32]{1,0:T(8,128)} fusion(f32[32,1024]{0,1:T(8,128)S(1)} %constant_dynamic-update-slice_fusion.5, s32[16384]{0:T(1024)S(1)} %broadcast_clamp_fusion.1), kind=kCustom, calls=%fused_computation.11 | custom fusion | bytes 4259840 | tf_op jit(solution)/shard_map/gather | solution.py:64
  378.9 54.4 %gather_fusion.10 = f32[16384,32]{1,0:T(8,128)} fusion(f32[32,1024]{0,1:T(8,128)S(1)} %constant_dynamic-update-slice_fusion.5, s32[16384]{0:T(1024)S(1)} %broadcast_clamp_fusion.2), kind=kCustom, calls=%fused_computation.10 | custom fusion | bytes 4259840 | tf_op jit(solution)/shard_map/gather | solution.py:64
  433.3 54.4 %gather_fusion.9 = f32[16384,32]{1,0:T(8,128)} fusion(f32[32,1024]{0,1:T(8,128)S(1)} %constant_dynamic-update-slice_fusion.5, s32[16384]{0:T(1024)S(1)} %broadcast_clamp_fusion.3), kind=kCustom, calls=%fused_computation.9 | custom fusion | bytes 4259840 | tf_op jit(solution)/shard_map/gather | solution.py:64
  487.7 54.3 %gather_fusion.8 = f32[16384,32]{1,0:T(8,128)} fusion(f32[32,1024]{0,1:T(8,128)S(1)} %constant_dynamic-update-slice_fusion.5, s32[16384]{0:T(1024)S(1)} %broadcast_clamp_fusion.4), kind=kCustom, calls=%fused_computation.8 | custom fusion | bytes 4259840 | tf_op jit(solution)/shard_map/gather | solution.py:64
  542.0 5.6 multiply_reduce_fusion
  547.6 5.4 multiply_reduce_fusion.1
  562.9 5.1 collective-permute-start.13
  591.6 5.1 collective-permute-start.19
  599.1 132.8 %all-gather.1 = f32[64,64,32]{1,2,0:T(8,128)S(1)} all-gather(f32[1,64,32]{1,2,0:T(8,128)S(1)} %convolution_bitcast_fusion.2), channel_id=1, replica_groups=mesh['rows'=64,'cols'=4] {'rows'}, dimensions={0}, use_global_device_ids=true | all-gather | bytes 532480 | tf_op jit(solution)/shard_map/all_gather | solution.py:49
  732.9 5.8 convolution_bitcast_fusion
  738.8 47.6 %reduce-scatter.9.cloned.1.call-done = f32[64,32]{1,0:T(8,128)} async-done(((f32[256,32]{1,0:T(8,128)}), f32[64,32]{1,0:T(8,128)}) %reduce-scatter.9.cloned.1.call-update) | async-done | bytes 8208
  787.5 6.0 fusion.7
  795.5 5.1 collective-permute-start.22
  807.4 4.8 collective-permute-done.20
  (158 shorter events, 92.4 us)
Async XLA Ops:
  7.2 213.9 %reduce-scatter.7.cloned.1.call-start = ((), (), s32[]{:S(2)}) async-start(), calls=%async_computation.2 | async-start | bytes 163840
  9.7 18.0 %collective-permute-start = (f32[32,128]{0,1:T(8,128)S(1)}, f32[32,128]{0,1:T(8,128)S(1)}, u32[]{:S(2)}, u32[]{:S(2)}) collective-permute-start(f32[32,128]{0,1:T(8,128)S(1)} %bitcast.186), channel_id=1, source_target_pairs={{0,4},{4,8},{8,12},{12,16},{16,20},{20,24},{24,28},{28,32},{32,36}... | collective-permute-start | bytes 49160 | tf_op jit(solution)/shard_map/ppermute | solution.py:10
  15.4 12.4 %collective-permute-start.1 = (f32[32,128]{0,1:T(8,128)S(1)}, f32[32,128]{0,1:T(8,128)S(1)}, u32[]{:S(2)}, u32[]{:S(2)}) collective-permute-start(f32[32,128]{0,1:T(8,128)S(1)} %bitcast.183), channel_id=1, source_target_pairs={{4,0},{8,4},{12,8},{16,12},{20,16},{24,20},{28,24},{32,28},{36,32}... | collective-permute-start | bytes 49160 | tf_op jit(solution)/shard_map/ppermute | solution.py:10
  18.0 9.9 %collective-permute-start.2 = (f32[32,128]{0,1:T(8,128)S(1)}, f32[32,128]{0,1:T(8,128)S(1)}, u32[]{:S(2)}, u32[]{:S(2)}) collective-permute-start(f32[32,128]{0,1:T(8,128)S(1)} %bitcast.184), channel_id=1, source_target_pairs={{0,1},{1,2},{2,3},{4,5},{5,6},{6,7},{8,9},{9,10},{10,11},{12,13},{... | collective-permute-start | bytes 49160 | tf_op jit(solution)/shard_map/ppermute | solution.py:10
  20.5 7.5 collective-permute-start.3
  171.7 614.8 %reduce-scatter.9.cloned.1.call-start = ((), (), s32[]{:S(2)}) async-start(), calls=%async_computation.3 | async-start | bytes 163840
  228.2 18.9 %collective-permute-start.7 = (f32[32,128]{1,0:T(8,128)S(1)}, f32[32,128]{1,0:T(8,128)S(1)}, u32[]{:S(2)}, u32[]{:S(2)}) collective-permute-start(f32[32,128]{1,0:T(8,128)S(1)} %get-tuple-element.28), channel_id=1, source_target_pairs={{0,1},{1,2},{2,3},{4,5},{5,6},{6,7},{8,9},{9,10},{10,11},{12,13},{... | collective-permute-start | bytes 49160 | tf_op jit(solution)/shard_map/ppermute | solution.py:10
  230.1 16.9 %collective-permute-start.6 = (f32[32,128]{1,0:T(8,128)S(1)}, f32[32,128]{1,0:T(8,128)S(1)}, u32[]{:S(2)}, u32[]{:S(2)}) collective-permute-start(f32[32,128]{1,0:T(8,128)S(1)} %get-tuple-element.29), channel_id=1, source_target_pairs={{1,0},{2,1},{3,2},{5,4},{6,5},{7,6},{9,8},{10,9},{11,10},{13,12},{... | collective-permute-start | bytes 49160 | tf_op jit(solution)/shard_map/ppermute | solution.py:10
  235.2 11.6 %collective-permute-start.5 = (f32[32,128]{1,0:T(8,128)S(1)}, f32[32,128]{1,0:T(8,128)S(1)}, u32[]{:S(2)}, u32[]{:S(2)}) collective-permute-start(f32[32,128]{1,0:T(8,128)S(1)} %get-tuple-element.30), channel_id=1, source_target_pairs={{0,4},{4,8},{8,12},{12,16},{16,20},{20,24},{24,28},{28,32},{32,36}... | collective-permute-start | bytes 49160 | tf_op jit(solution)/shard_map/ppermute | solution.py:10
  253.3 15.1 %collective-permute-start.8 = (f32[32,128]{0,1:T(8,128)S(1)}, f32[32,128]{0,1:T(8,128)S(1)}, u32[]{:S(2)}, u32[]{:S(2)}) collective-permute-start(f32[32,128]{0,1:T(8,128)S(1)} %bitcast.191), channel_id=1, source_target_pairs={{0,4},{4,8},{8,12},{12,16},{16,20},{20,24},{24,28},{28,32},{32,36}... | collective-permute-start | bytes 49160 | tf_op jit(solution)/shard_map/ppermute | solution.py:10
  257.2 11.2 %collective-permute-start.9 = (f32[32,128]{0,1:T(8,128)S(1)}, f32[32,128]{0,1:T(8,128)S(1)}, u32[]{:S(2)}, u32[]{:S(2)}) collective-permute-start(f32[32,128]{0,1:T(8,128)S(1)} %bitcast.193), channel_id=1, source_target_pairs={{4,0},{8,4},{12,8},{16,12},{20,16},{24,20},{28,24},{32,28},{36,32}... | collective-permute-start | bytes 49160 | tf_op jit(solution)/shard_map/ppermute | solution.py:10
  261.1 7.3 collective-permute-start.10
  263.1 7.0 collective-permute-start.11
  561.0 13.7 %collective-permute-start.12 = (f32[32,128]{0,1:T(8,128)S(1)}, f32[32,128]{0,1:T(8,128)S(1)}, u32[]{:S(2)}, u32[]{:S(2)}) collective-permute-start(f32[32,128]{0,1:T(8,128)S(1)} %get-tuple-element.13), channel_id=1, source_target_pairs={{4,0},{8,4},{12,8},{16,12},{20,16},{24,20},{28,24},{32,28},{36,32}... | collective-permute-start | bytes 49160 | tf_op jit(solution)/shard_map/ppermute | solution.py:10
  562.9 13.1 %collective-permute-start.13 = (f32[32,128]{0,1:T(8,128)S(1)}, f32[32,128]{0,1:T(8,128)S(1)}, u32[]{:S(2)}, u32[]{:S(2)}) collective-permute-start(f32[32,128]{0,1:T(8,128)S(1)} %get-tuple-element.12), channel_id=1, source_target_pairs={{0,4},{4,8},{8,12},{12,16},{16,20},{20,24},{24,28},{28,32},{32,36}... | collective-permute-start | bytes 49160 | tf_op jit(solution)/shard_map/ppermute | solution.py:10
  568.0 9.4 %collective-permute-start.14 = (f32[32,128]{0,1:T(8,128)S(1)}, f32[32,128]{0,1:T(8,128)S(1)}, u32[]{:S(2)}, u32[]{:S(2)}) collective-permute-start(f32[32,128]{0,1:T(8,128)S(1)} %get-tuple-element.11), channel_id=1, source_target_pairs={{1,0},{2,1},{3,2},{5,4},{6,5},{7,6},{9,8},{10,9},{11,10},{13,12},{... | collective-permute-start | bytes 49160 | tf_op jit(solution)/shard_map/ppermute | solution.py:10
  572.7 7.1 collective-permute-start.15
  583.9 13.0 %collective-permute-start.16 = (f32[32,128]{0,1:T(8,128)S(1)}, f32[32,128]{0,1:T(8,128)S(1)}, u32[]{:S(2)}, u32[]{:S(2)}) collective-permute-start(f32[32,128]{0,1:T(8,128)S(1)} %bitcast.192), channel_id=1, source_target_pairs={{0,4},{4,8},{8,12},{12,16},{16,20},{20,24},{24,28},{28,32},{32,36}... | collective-permute-start | bytes 49160 | tf_op jit(solution)/shard_map/ppermute | solution.py:10
  586.1 10.8 %collective-permute-start.17 = (f32[32,128]{0,1:T(8,128)S(1)}, f32[32,128]{0,1:T(8,128)S(1)}, u32[]{:S(2)}, u32[]{:S(2)}) collective-permute-start(f32[32,128]{0,1:T(8,128)S(1)} %bitcast.189), channel_id=1, source_target_pairs={{4,0},{8,4},{12,8},{16,12},{20,16},{24,20},{28,24},{32,28},{36,32}... | collective-permute-start | bytes 49160 | tf_op jit(solution)/shard_map/ppermute | solution.py:10
  589.7 7.3 collective-permute-start.18
  591.6 7.0 collective-permute-start.19
  793.6 18.9 %collective-permute-start.23 = (f32[32,128]{1,0:T(8,128)S(1)}, f32[32,128]{1,0:T(8,128)S(1)}, u32[]{:S(2)}, u32[]{:S(2)}) collective-permute-start(f32[32,128]{1,0:T(8,128)S(1)} %get-tuple-element.24), channel_id=1, source_target_pairs={{0,1},{1,2},{2,3},{4,5},{5,6},{6,7},{8,9},{9,10},{10,11},{12,13},{... | collective-permute-start | bytes 49160 | tf_op jit(solution)/shard_map/ppermute | solution.py:10
  795.5 16.9 %collective-permute-start.22 = (f32[32,128]{1,0:T(8,128)S(1)}, f32[32,128]{1,0:T(8,128)S(1)}, u32[]{:S(2)}, u32[]{:S(2)}) collective-permute-start(f32[32,128]{1,0:T(8,128)S(1)} %get-tuple-element.25), channel_id=1, source_target_pairs={{1,0},{2,1},{3,2},{5,4},{6,5},{7,6},{9,8},{10,9},{11,10},{13,12},{... | collective-permute-start | bytes 49160 | tf_op jit(solution)/shard_map/ppermute | solution.py:10
  800.6 11.6 %collective-permute-start.21 = (f32[32,128]{1,0:T(8,128)S(1)}, f32[32,128]{1,0:T(8,128)S(1)}, u32[]{:S(2)}, u32[]{:S(2)}) collective-permute-start(f32[32,128]{1,0:T(8,128)S(1)} %get-tuple-element.26), channel_id=1, source_target_pairs={{0,4},{4,8},{8,12},{12,16},{16,20},{20,24},{24,28},{28,32},{32,36}... | collective-permute-start | bytes 49160 | tf_op jit(solution)/shard_map/ppermute | solution.py:10
  (11 other events, 512.3 us)
Sparse Core Ops, SparseCore 0:
  171.8 49.2 reduce-scatter.6
  738.8 47.5 reduce-scatter.8
where the time goes:
time: 827 us; the launch traced here: 826 us
  local copies, waits for them, and re-layouts  286 us (35%)
  blocking collectives  269 us (33%)
  waiting for transfers between devices  111 us (13%)
  starting transfers between devices  81 us (10%)
  other arithmetic  37.1 us (4%)
  matrix products  26.4 us (3%)
  between operations  15 us (2%)
    gather x5, local copies, waits for them, and re-layouts, couple(): nearby = sub[:, index[begin:finish]]  272 us
    all_gather x2, blocking collectives, coarse_apply(): lax.all_gather(restricted, 'rows', axis=1, tiled=True)  269 us
    unnamed x4, waiting for transfers between devices  96.9 us
    ppermute x24, starting transfers between devices, from_behind(): return lax.ppermute(block, axis, route)  80.9 us
    reduce_sum x5, other arithmetic, couple(): coupled = coupled + jnp.sum(nearby * coef[None, begin:finish, :], axis=1)  18.5 us
  transfers between devices with their start and end apart: 26, of which 7 were waited for; matrix products, arithmetic and copies ran while one was open for 1% of the time, Pallas kernels for 0%

commit v1 on v0

--- a/solution.py
+++ b/solution.py
@@ -46,7 +46,9 @@
 def coarse_apply(restricted, coarse_block):
     highest = lax.Precision.HIGHEST
     partial_sum = lax.dot_general(
-        lax.all_gather(restricted, "rows", axis=1, tiled=True),
+        jnp.concatenate(
+            lax.all_to_all(jnp.stack([restricted] * lax.axis_size("rows")), "rows", 0, 0), axis=1
+        ),
         coarse_block,
         (((1,), (1,)), ((), ())),
         precision=highest,

time: 827 us -> 574 us (0.69)
  blocking collectives: 269 us -> 22.3 us
  waiting for transfers between devices: 111 us -> 82.2 us
  starting transfers between devices: 81 us -> 92.5 us
    all_gather x2 -> x0, blocking collectives: 269 us -> none  [coarse_apply(): lax.all_gather(restricted, 'rows', axis=1, tiled=True)]
    unnamed x4, waiting for transfers between devices: 96.9 us -> 57 us
    all_to_all x0 -> x1, blocking collectives: none -> 22.3 us  [coarse_apply(): lax.all_to_all(jnp.stack([restricted] * lax.axis_size('rows')), 'rows', 0...]
    all_to_all x0 -> x1, waiting for transfers between devices: none -> 12.1 us  [coarse_apply(): lax.all_to_all(jnp.stack([restricted] * lax.axis_size('rows')), 'rows', 0...]
    all_to_all x0 -> x1, starting transfers between devices: none -> 11.7 us  [coarse_apply(): lax.all_to_all(jnp.stack([restricted] * lax.axis_size('rows')), 'rows', 0...]
  transfers between devices with their start and end apart: 26 -> 27, of which waited for: 7 -> 8; matrix products, arithmetic and copies ran while one was open for 1% -> 2% of each run, Pallas kernels for 0% -> 0%
where the time goes in v1:
time: 574 us; the launch traced here: 573 us
  local copies, waits for them, and re-layouts  292 us (51%)
  starting transfers between devices  92.5 us (16%)
  waiting for transfers between devices  82.2 us (14%)
  other arithmetic  42.2 us (7%)
  matrix products  26.5 us (5%)
  blocking collectives  22.3 us (4%)
  between operations  15.1 us (3%)
    gather x5, local copies, waits for them, and re-layouts, couple(): nearby = sub[:, index[begin:finish]]  272 us
    ppermute x24, starting transfers between devices, from_behind(): return lax.ppermute(block, axis, route)  80.7 us
    unnamed x4, waiting for transfers between devices  57 us
    all_to_all x1, blocking collectives, coarse_apply(): lax.all_to_all(jnp.stack([restricted] * lax.axis_size('rows')), 'rows', 0...  22.3 us
    reduce_sum x5, other arithmetic, couple(): coupled = coupled + jnp.sum(nearby * coef[None, begin:finish, :], axis=1)  18.5 us
    scatter-add x12, other arithmetic, fold(): owned = owned.at[:, sends[e]].add(backs[e])  16.6 us
    ppermute x24, waiting for transfers between devices, from_behind(): return lax.ppermute(block, axis, route)  13.1 us
    all_to_all x1, waiting for transfers between devices, coarse_apply(): lax.all_to_all(jnp.stack([restricted] * lax.axis_size('rows')), 'rows', 0...  12.1 us
  transfers between devices with their start and end apart: 27, of which 8 were waited for; matrix products, arithmetic and copies ran while one was open for 2% of the time, Pallas kernels for 0%

profile of v1, /device:TPU:120, one launch (start us, length us, event | category | flops | bytes accessed | tf_op | source)
XLA Modules:
  0.0 572.5 jit_solution(10815104249092816097)
XLA Ops:
  9.7 5.0 collective-permute-start
  20.5 5.1 collective-permute-start.3
  29.9 11.7 %all-to-all-start = ((f32[64,1,2048]{2,1,0:T(1,128)}), f32[64,1,2048]{2,1,0:T(1,128)S(1)}, u32[]{:S(2)}, u32[]{:S(2)}) async-start(f32[64,1,2048]{2,1,0:T(1,128)} %reshape.554), calls=%async_computation | async-start | bytes 1048576 | tf_op jit(solution)/shard_map/all_to_all | solution.py:50
  43.0 12.1 %all-to-all-done = f32[64,1,2048]{2,1,0:T(1,128)S(1)} async-done(((f32[64,1,2048]{2,1,0:T(1,128)}), f32[64,1,2048]{2,1,0:T(1,128)S(1)}, u32[]{:S(2)}, u32[]{:S(2)}) %all-to-all-start) | async-done | bytes 524320 | tf_op jit(solution)/shard_map/all_to_all | solution.py:50
  59.0 5.8 %convolution_bitcast_fusion.1 = f32[256,32]{1,0:T(8,128)} fusion(f32[32,4096]{1,0:T(8,128)S(1)} %reshape.302, f32[256,4096]{1,0:T(8,128)} %param.11), kind=kOutput, calls=%fused_computation.41 | convolution fusion | flops 402653184 | bytes 4751360
  64.9 28.4 %reduce-scatter.7.cloned.1.call-done = f32[64,32]{1,0:T(8,128)} async-done(((f32[256,32]{1,0:T(8,128)}), f32[64,32]{1,0:T(8,128)}) %reduce-scatter.7.cloned.1.call-update) | async-done | bytes 8208
  94.3 6.0 %fusion.4 = f32[32,1024]{1,0:T(8,128)S(1)} fusion(f32[32,1024]{1,0:T(8,128)S(1)} %fusion.14, f32[32,1024]{1,0:T(8,128)S(1)} %constant_dynamic-update-slice_fusion, f32[1,1,1024,1024]{3,2,1,0:T(8,128)} %param.9), kind=kOutput, calls=%fused_computation.38 | convolution fusion | flops 402685952 | bytes 4587520 | tf_op jit(solution)/shard_map/dot_general | solution.py:86
  102.3 5.1 collective-permute-start.6
  135.9 5.1 collective-permute-start.11
  143.0 54.4 %gather_fusion.12 = f32[16384,32]{1,0:T(8,128)} fusion(f32[32,1024]{0,1:T(8,128)S(1)} %constant_dynamic-update-slice_fusion.5, s32[16384]{0:T(1024)S(1)} %copy-done.3), kind=kCustom, calls=%fused_computation.12 | custom fusion | bytes 4259840 | tf_op jit(solution)/shard_map/gather | solution.py:66
  197.4 54.4 %gather_fusion.11 = f32[16384,32]{1,0:T(8,128)} fusion(f32[32,1024]{0,1:T(8,128)S(1)} %constant_dynamic-update-slice_fusion.5, s32[16384]{0:T(1024)S(1)} %broadcast_clamp_fusion.1), kind=kCustom, calls=%fused_computation.11 | custom fusion | bytes 4259840 | tf_op jit(solution)/shard_map/gather | solution.py:66
  251.8 54.4 %gather_fusion.10 = f32[16384,32]{1,0:T(8,128)} fusion(f32[32,1024]{0,1:T(8,128)S(1)} %constant_dynamic-update-slice_fusion.5, s32[16384]{0:T(1024)S(1)} %broadcast_clamp_fusion.2), kind=kCustom, calls=%fused_computation.10 | custom fusion | bytes 4259840 | tf_op jit(solution)/shard_map/gather | solution.py:66
  306.2 54.4 %gather_fusion.9 = f32[16384,32]{1,0:T(8,128)} fusion(f32[32,1024]{0,1:T(8,128)S(1)} %constant_dynamic-update-slice_fusion.5, s32[16384]{0:T(1024)S(1)} %copy-done.2), kind=kCustom, calls=%fused_computation.9 | custom fusion | bytes 4259840 | tf_op jit(solution)/shard_map/gather | solution.py:66
  360.6 54.3 %gather_fusion.8 = f32[16384,32]{1,0:T(8,128)} fusion(f32[32,1024]{0,1:T(8,128)S(1)} %constant_dynamic-update-slice_fusion.5, s32[16384]{0:T(1024)S(1)} %broadcast_clamp_fusion.4), kind=kCustom, calls=%fused_computation.8 | custom fusion | bytes 4259840 | tf_op jit(solution)/shard_map/gather | solution.py:66
  414.9 5.6 multiply_reduce_fusion
  420.5 5.4 multiply_reduce_fusion.1
  435.8 5.1 collective-permute-start.13
  465.0 5.1 collective-permute-start.19
  473.3 22.3 %all_to_all.10 = f32[64,1,2048]{2,1,0:T(1,128)S(1)} all-to-all(f32[64,1,2048]{2,1,0:T(1,128)S(1)} %reshape.556), channel_id=1, replica_groups=mesh['rows'=64,'cols'=4] {'rows'}, dimensions={0} | all-to-all | bytes 1048576 | tf_op jit(solution)/shard_map/all_to_all | solution.py:50
  498.8 5.8 %convolution_bitcast_fusion = f32[256,32]{1,0:T(8,128)} fusion(f32[32,4096]{1,0:T(8,128)S(1)} %reshape.304, f32[256,4096]{1,0:T(8,128)} %param.11), kind=kOutput, calls=%fused_computation.40 | convolution fusion | flops 402653184 | bytes 4751360
  504.7 28.6 %reduce-scatter.9.cloned.1.call-done = f32[64,32]{1,0:T(8,128)} async-done(((f32[256,32]{1,0:T(8,128)}), f32[64,32]{1,0:T(8,128)}) %reduce-scatter.9.cloned.1.call-update) | async-done | bytes 8208
  534.4 6.0 %fusion.7 = f32[32,1024]{1,0:T(8,128)S(1)} fusion(f32[32,1024]{1,0:T(8,128)S(1)} %fusion.10, f32[32,1024]{1,0:T(8,128)S(1)} %constant_dynamic-update-slice_fusion.10, f32[1,1,1024,1024]{3,2,1,0:T(8,128)} %param.9), kind=kOutput, calls=%fused_computation.39 | convolution fusion | flops 402685952 | bytes 4587520 | tf_op jit(solution)/shard_map/dot_general | solution.py:86
  542.4 5.1 collective-permute-start.22
  554.3 4.8 collective-permute-done.20
  (178 shorter events, 107.2 us)
Async XLA Ops:
  9.7 18.0 %collective-permute-start = (f32[32,128]{0,1:T(8,128)S(1)}, f32[32,128]{0,1:T(8,128)S(1)}, u32[]{:S(2)}, u32[]{:S(2)}) collective-permute-start(f32[32,128]{0,1:T(8,128)S(1)} %bitcast.179), channel_id=1, source_target_pairs={{0,4},{4,8},{8,12},{12,16},{16,20},{20,24},{24,28},{28,32},{32,36}... | collective-permute-start | bytes 49160 | tf_op jit(solution)/shard_map/ppermute | solution.py:10
  15.3 12.4 %collective-permute-start.1 = (f32[32,128]{0,1:T(8,128)S(1)}, f32[32,128]{0,1:T(8,128)S(1)}, u32[]{:S(2)}, u32[]{:S(2)}) collective-permute-start(f32[32,128]{0,1:T(8,128)S(1)} %bitcast.177), channel_id=1, source_target_pairs={{4,0},{8,4},{12,8},{16,12},{20,16},{24,20},{28,24},{32,28},{36,32}... | collective-permute-start | bytes 49160 | tf_op jit(solution)/shard_map/ppermute | solution.py:10
  18.0 9.8 %collective-permute-start.2 = (f32[32,128]{0,1:T(8,128)S(1)}, f32[32,128]{0,1:T(8,128)S(1)}, u32[]{:S(2)}, u32[]{:S(2)}) collective-permute-start(f32[32,128]{0,1:T(8,128)S(1)} %bitcast.178), channel_id=1, source_target_pairs={{0,1},{1,2},{2,3},{4,5},{5,6},{6,7},{8,9},{9,10},{10,11},{12,13},{... | collective-permute-start | bytes 49160 | tf_op jit(solution)/shard_map/ppermute | solution.py:10
  20.5 7.3 %collective-permute-start.3 = (f32[32,128]{0,1:T(8,128)S(1)}, f32[32,128]{0,1:T(8,128)S(1)}, u32[]{:S(2)}, u32[]{:S(2)}) collective-permute-start(f32[32,128]{0,1:T(8,128)S(1)} %bitcast.175), channel_id=1, source_target_pairs={{1,0},{2,1},{3,2},{5,4},{6,5},{7,6},{9,8},{10,9},{11,10},{13,12},{... | collective-permute-start | bytes 49160 | tf_op jit(solution)/shard_map/ppermute | solution.py:10
  29.9 25.2 %all-to-all-start = ((f32[64,1,2048]{2,1,0:T(1,128)}), f32[64,1,2048]{2,1,0:T(1,128)S(1)}, u32[]{:S(2)}, u32[]{:S(2)}) async-start(f32[64,1,2048]{2,1,0:T(1,128)} %reshape.554), calls=%async_computation | async-start | bytes 1048576 | tf_op jit(solution)/shard_map/all_to_all | solution.py:50
  41.6 51.7 %reduce-scatter.7.cloned.1.call-start = ((), (), s32[]{:S(2)}) async-start(), calls=%async_computation.4 | async-start | bytes 163840
  64.8 468.5 %reduce-scatter.9.cloned.1.call-start = ((), (), s32[]{:S(2)}) async-start(), calls=%async_computation.5 | async-start | bytes 163840
  100.4 18.9 %collective-permute-start.7 = (f32[32,128]{1,0:T(8,128)S(1)}, f32[32,128]{1,0:T(8,128)S(1)}, u32[]{:S(2)}, u32[]{:S(2)}) collective-permute-start(f32[32,128]{1,0:T(8,128)S(1)} %get-tuple-element.28), channel_id=1, source_target_pairs={{0,1},{1,2},{2,3},{4,5},{5,6},{6,7},{8,9},{9,10},{10,11},{12,13},{... | collective-permute-start | bytes 49160 | tf_op jit(solution)/shard_map/ppermute | solution.py:10
  102.3 16.9 %collective-permute-start.6 = (f32[32,128]{1,0:T(8,128)S(1)}, f32[32,128]{1,0:T(8,128)S(1)}, u32[]{:S(2)}, u32[]{:S(2)}) collective-permute-start(f32[32,128]{1,0:T(8,128)S(1)} %get-tuple-element.29), channel_id=1, source_target_pairs={{1,0},{2,1},{3,2},{5,4},{6,5},{7,6},{9,8},{10,9},{11,10},{13,12},{... | collective-permute-start | bytes 49160 | tf_op jit(solution)/shard_map/ppermute | solution.py:10
  107.5 11.6 %collective-permute-start.5 = (f32[32,128]{1,0:T(8,128)S(1)}, f32[32,128]{1,0:T(8,128)S(1)}, u32[]{:S(2)}, u32[]{:S(2)}) collective-permute-start(f32[32,128]{1,0:T(8,128)S(1)} %get-tuple-element.30), channel_id=1, source_target_pairs={{0,4},{4,8},{8,12},{12,16},{16,20},{20,24},{24,28},{28,32},{32,36}... | collective-permute-start | bytes 49160 | tf_op jit(solution)/shard_map/ppermute | solution.py:10
  125.8 15.3 %collective-permute-start.8 = (f32[32,128]{0,1:T(8,128)S(1)}, f32[32,128]{0,1:T(8,128)S(1)}, u32[]{:S(2)}, u32[]{:S(2)}) collective-permute-start(f32[32,128]{0,1:T(8,128)S(1)} %bitcast.183), channel_id=1, source_target_pairs={{0,4},{4,8},{8,12},{12,16},{16,20},{20,24},{24,28},{28,32},{32,36}... | collective-permute-start | bytes 49160 | tf_op jit(solution)/shard_map/ppermute | solution.py:10
  130.1 11.0 %collective-permute-start.9 = (f32[32,128]{0,1:T(8,128)S(1)}, f32[32,128]{0,1:T(8,128)S(1)}, u32[]{:S(2)}, u32[]{:S(2)}) collective-permute-start(f32[32,128]{0,1:T(8,128)S(1)} %bitcast.185), channel_id=1, source_target_pairs={{4,0},{8,4},{12,8},{16,12},{20,16},{24,20},{28,24},{32,28},{36,32}... | collective-permute-start | bytes 49160 | tf_op jit(solution)/shard_map/ppermute | solution.py:10
  134.0 7.1 %collective-permute-start.10 = (f32[32,128]{0,1:T(8,128)S(1)}, f32[32,128]{0,1:T(8,128)S(1)}, u32[]{:S(2)}, u32[]{:S(2)}) collective-permute-start(f32[32,128]{0,1:T(8,128)S(1)} %bitcast.182), channel_id=1, source_target_pairs={{0,1},{1,2},{2,3},{4,5},{5,6},{6,7},{8,9},{9,10},{10,11},{12,13},{... | collective-permute-start | bytes 49160 | tf_op jit(solution)/shard_map/ppermute | solution.py:10
  433.8 13.7 %collective-permute-start.12 = (f32[32,128]{0,1:T(8,128)S(1)}, f32[32,128]{0,1:T(8,128)S(1)}, u32[]{:S(2)}, u32[]{:S(2)}) collective-permute-start(f32[32,128]{0,1:T(8,128)S(1)} %get-tuple-element.13), channel_id=1, source_target_pairs={{4,0},{8,4},{12,8},{16,12},{20,16},{24,20},{28,24},{32,28},{36,32}... | collective-permute-start | bytes 49160 | tf_op jit(solution)/shard_map/ppermute | solution.py:10
  435.8 13.1 %collective-permute-start.13 = (f32[32,128]{0,1:T(8,128)S(1)}, f32[32,128]{0,1:T(8,128)S(1)}, u32[]{:S(2)}, u32[]{:S(2)}) collective-permute-start(f32[32,128]{0,1:T(8,128)S(1)} %get-tuple-element.12), channel_id=1, source_target_pairs={{0,4},{4,8},{8,12},{12,16},{16,20},{20,24},{24,28},{28,32},{32,36}... | collective-permute-start | bytes 49160 | tf_op jit(solution)/shard_map/ppermute | solution.py:10
  440.9 9.4 %collective-permute-start.14 = (f32[32,128]{0,1:T(8,128)S(1)}, f32[32,128]{0,1:T(8,128)S(1)}, u32[]{:S(2)}, u32[]{:S(2)}) collective-permute-start(f32[32,128]{0,1:T(8,128)S(1)} %get-tuple-element.11), channel_id=1, source_target_pairs={{1,0},{2,1},{3,2},{5,4},{6,5},{7,6},{9,8},{10,9},{11,10},{13,12},{... | collective-permute-start | bytes 49160 | tf_op jit(solution)/shard_map/ppermute | solution.py:10
  445.6 7.1 %collective-permute-start.15 = (f32[32,128]{0,1:T(8,128)S(1)}, f32[32,128]{0,1:T(8,128)S(1)}, u32[]{:S(2)}, u32[]{:S(2)}) collective-permute-start(f32[32,128]{0,1:T(8,128)S(1)} %get-tuple-element.10), channel_id=1, source_target_pairs={{0,1},{1,2},{2,3},{4,5},{5,6},{6,7},{8,9},{9,10},{10,11},{12,13},{... | collective-permute-start | bytes 49160 | tf_op jit(solution)/shard_map/ppermute | solution.py:10
  457.2 13.0 %collective-permute-start.16 = (f32[32,128]{0,1:T(8,128)S(1)}, f32[32,128]{0,1:T(8,128)S(1)}, u32[]{:S(2)}, u32[]{:S(2)}) collective-permute-start(f32[32,128]{0,1:T(8,128)S(1)} %bitcast.184), channel_id=1, source_target_pairs={{0,4},{4,8},{8,12},{12,16},{16,20},{20,24},{24,28},{28,32},{32,36}... | collective-permute-start | bytes 49160 | tf_op jit(solution)/shard_map/ppermute | solution.py:10
  459.4 10.8 %collective-permute-start.17 = (f32[32,128]{0,1:T(8,128)S(1)}, f32[32,128]{0,1:T(8,128)S(1)}, u32[]{:S(2)}, u32[]{:S(2)}) collective-permute-start(f32[32,128]{0,1:T(8,128)S(1)} %bitcast.181), channel_id=1, source_target_pairs={{4,0},{8,4},{12,8},{16,12},{20,16},{24,20},{28,24},{32,28},{36,32}... | collective-permute-start | bytes 49160 | tf_op jit(solution)/shard_map/ppermute | solution.py:10
  463.1 7.3 %collective-permute-start.18 = (f32[32,128]{0,1:T(8,128)S(1)}, f32[32,128]{0,1:T(8,128)S(1)}, u32[]{:S(2)}, u32[]{:S(2)}) collective-permute-start(f32[32,128]{0,1:T(8,128)S(1)} %bitcast.176), channel_id=1, source_target_pairs={{0,1},{1,2},{2,3},{4,5},{5,6},{6,7},{8,9},{9,10},{10,11},{12,13},{... | collective-permute-start | bytes 49160 | tf_op jit(solution)/shard_map/ppermute | solution.py:10
  465.0 7.0 %collective-permute-start.19 = (f32[32,128]{0,1:T(8,128)S(1)}, f32[32,128]{0,1:T(8,128)S(1)}, u32[]{:S(2)}, u32[]{:S(2)}) collective-permute-start(f32[32,128]{0,1:T(8,128)S(1)} %bitcast.174), channel_id=1, source_target_pairs={{1,0},{2,1},{3,2},{5,4},{6,5},{7,6},{9,8},{10,9},{11,10},{13,12},{... | collective-permute-start | bytes 49160 | tf_op jit(solution)/shard_map/ppermute | solution.py:10
  540.4 18.9 %collective-permute-start.23 = (f32[32,128]{1,0:T(8,128)S(1)}, f32[32,128]{1,0:T(8,128)S(1)}, u32[]{:S(2)}, u32[]{:S(2)}) collective-permute-start(f32[32,128]{1,0:T(8,128)S(1)} %get-tuple-element.24), channel_id=1, source_target_pairs={{0,1},{1,2},{2,3},{4,5},{5,6},{6,7},{8,9},{9,10},{10,11},{12,13},{... | collective-permute-start | bytes 49160 | tf_op jit(solution)/shard_map/ppermute | solution.py:10
  542.4 16.9 %collective-permute-start.22 = (f32[32,128]{1,0:T(8,128)S(1)}, f32[32,128]{1,0:T(8,128)S(1)}, u32[]{:S(2)}, u32[]{:S(2)}) collective-permute-start(f32[32,128]{1,0:T(8,128)S(1)} %get-tuple-element.25), channel_id=1, source_target_pairs={{1,0},{2,1},{3,2},{5,4},{6,5},{7,6},{9,8},{10,9},{11,10},{13,12},{... | collective-permute-start | bytes 49160 | tf_op jit(solution)/shard_map/ppermute | solution.py:10
  547.5 11.6 %collective-permute-start.21 = (f32[32,128]{1,0:T(8,128)S(1)}, f32[32,128]{1,0:T(8,128)S(1)}, u32[]{:S(2)}, u32[]{:S(2)}) collective-permute-start(f32[32,128]{1,0:T(8,128)S(1)} %get-tuple-element.26), channel_id=1, source_target_pairs={{0,4},{4,8},{8,12},{12,16},{16,20},{20,24},{24,28},{28,32},{32,36}... | collective-permute-start | bytes 49160 | tf_op jit(solution)/shard_map/ppermute | solution.py:10
  (17 other events, 337.1 us)
Sparse Core Ops, SparseCore 0:
  64.9 28.2 reduce-scatter.6
  504.7 28.5 reduce-scatter.8
